TPU v7x, 32 devices: a whole 2x2x4 slice. The times are simulated.
32 devices in a mesh: kpt: 2 (over y), pert: 4 (over z), pw: 4 (over x, core).
Axes of the slice: x: 2, y: 2, z: 4, core: 2. Of those that a mesh axis runs over, the one named last changes fastest.
Arguments:
- occupied: bfloat16 [3072, 8192], P(('kpt', 'pert'), 'pw'), parts along dimension 0, may hold values from -0.0625 to 0.0625
- response: bfloat16 [8, 128, 8192], P(('kpt', 'pert'), None, 'pw'), parts along dimension 0, may hold values from -6 to 6
Outputs:
- correlation: float32 [8, 128, 1536], P(('kpt', 'pert')), parts along dimension 0
- projected: float32 [8, 128, 8192], P(('kpt', 'pert'), None, 'pw'), parts along dimension 0
There are 2 independent parts, one for each index of `kpt`. A program takes and returns all parts, laid end to end along the dimension named above; each array names one. Nothing has to cross between parts.
All inputs are finite; a program needn't handle non-finite values.
Results may differ from a plain program's by a relative error of at most 0.00096.
Values may be sent and summed in bfloat16 or wider, within the bound.
A program may use at most 64 MiB of HBM per device.

v0:
```python
import jax
import jax.numpy as jnp
from jax import lax
from jax.sharding import PartitionSpec as P


def from_behind(block, axis, distance):
    devices = range(lax.axis_size(axis))
    route = [((i - distance) % len(devices), i) for i in devices]
    return lax.ppermute(block, axis, route)


def local(occupied, response):
    rows = response.reshape(-1, response.shape[-1])
    band_local = occupied.shape[0]
    cycle_size = lax.axis_size("pert")
    total_bands = band_local * cycle_size
    zero_index = jnp.zeros((), jnp.int32)
    empty_correlation = jnp.zeros((rows.shape[0], total_bands), jnp.float32)
    empty_correction = jnp.zeros(rows.shape, jnp.float32)
    position = lax.axis_index("pert")

    def visit(step, piece, correlation, correction):
        owner = (position - step) % cycle_size
        start = owner * band_local
        part = lax.dot_general(
            rows, piece, (((1,), (1,)), ((), ())), preferred_element_type=jnp.float32
        )
        summed = lax.psum(part, "pw")
        correlation = lax.dynamic_update_slice(correlation, summed, (zero_index, start))
        correction = correction + jnp.dot(
            summed.astype(jnp.bfloat16), piece, preferred_element_type=jnp.float32
        )
        return (correlation, correction)

    def turn(step, state):
        piece, correlation, correction = state
        correlation, correction = visit(step, piece, correlation, correction)
        piece = from_behind(piece, "pert", 1)
        return (piece, correlation, correction)

    piece, correlation, correction = lax.fori_loop(
        0, cycle_size - 1, turn, (occupied, empty_correlation, empty_correction)
    )
    correlation, correction = visit(cycle_size - 1, piece, correlation, correction)
    projected = rows.astype(jnp.float32) - correction
    correlation_out = correlation.reshape(response.shape[0], response.shape[1], total_bands)
    return (correlation_out, projected.reshape(response.shape))


def solution(mesh):
    in_specs = (P(("kpt", "pert"), "pw"), P(("kpt", "pert"), None, "pw"))
    out_specs = (P(("kpt", "pert"), None, None), P(("kpt", "pert"), None, "pw"))
    return jax.shard_map(local, mesh=mesh, in_specs=in_specs, out_specs=out_specs, check_vma=False)
```

profile of v0, /device:TPU:30, one launch (start us, length us, event | category | flops | bytes accessed | tf_op | source)
XLA Modules:
  0.0 172.9 jit_solution(3041188094833959325)
XLA Ops:
  8.0 1.0 broadcast_in_dim.6
  9.0 0.7 copy-done
  9.7 117.6 %while.20 = (s32[]{:T(128)}, bf16[384,2048]{1,0:T(8,128)(2,1)S(1)}, f32[128,1536]{1,0:T(8,128)}, f32[128,2048]{1,0:T(8,128)}, bf16[128,2048]{1,0:T(8,128)(2,1)},...) while((s32[]{:T(128)}, bf16[384,2048]{1,0:T(8,128)(2,1)S(1)}, ...), condition=%wide.region_2.3_spmd.clone, body=%wide.region_0.2_spmd.clone.sunk | while | flops 403275776 | bytes 19267988 | solution.py:42
  10.1 0.6 copy-done.2
  10.7 1.3 fusion.20
  12.1 32.5 %all-reduce.5.cloned.1.call-done = f32[128,384]{1,0:T(8,128)} async-done(((f32[128,384]{1,0:T(8,128)}), f32[128,384]{1,0:T(8,128)}) %all-reduce.5.cloned.1.call-update) | async-done | bytes 196624 | tf_op jit(solution)/shard_map/while/body/eval_jaxpr/psum | solution.py:29
  44.6 1.6 constant_dynamic-update-slice_fusion.3
  46.2 2.3 %convolution_add_fusion.3 = f32[128,2048]{1,0:T(8,128)} fusion(bf16[384,2048]{1,0:T(8,128)(2,1)S(1)} %copy.12, f32[128,2048]{1,0:T(8,128)} %get-tuple-element.247, pred[]{:T(512)S(6)} %compare.5, f32[128,384]{1,0:T(8,128)} %all-reduce.5.cloned.1.call-done), kind=kOutput, calls=%fused_computation.clone.1 | convolution fusion | flops 201900032 | bytes 3866625 | tf_op jit(solution)/shard_map/while/body/eval_jaxpr/dot_general | solution.py:31
  48.7 0.5 collective-permute-start
  49.6 1.3 fusion.20
  51.0 32.6 %all-reduce.5.cloned.1.call-done = f32[128,384]{1,0:T(8,128)} async-done(((f32[128,384]{1,0:T(8,128)}), f32[128,384]{1,0:T(8,128)}) %all-reduce.5.cloned.1.call-update) | async-done | bytes 196624 | tf_op jit(solution)/shard_map/while/body/eval_jaxpr/psum | solution.py:29
  83.6 1.6 constant_dynamic-update-slice_fusion.3
  85.2 2.8 %convolution_add_fusion.3 = f32[128,2048]{1,0:T(8,128)} fusion(bf16[384,2048]{1,0:T(8,128)(2,1)S(1)} %copy.12, f32[128,2048]{1,0:T(8,128)} %get-tuple-element.247, pred[]{:T(512)S(6)} %compare.5, f32[128,384]{1,0:T(8,128)} %all-reduce.5.cloned.1.call-done), kind=kOutput, calls=%fused_computation.clone.1 | convolution fusion | flops 201900032 | bytes 3866625 | tf_op jit(solution)/shard_map/while/body/eval_jaxpr/dot_general | solution.py:31
  88.1 0.5 collective-permute-start
  88.7 0.3 copy-done.2
  89.0 1.3 fusion.20
  90.3 32.6 %all-reduce.5.cloned.1.call-done = f32[128,384]{1,0:T(8,128)} async-done(((f32[128,384]{1,0:T(8,128)}), f32[128,384]{1,0:T(8,128)}) %all-reduce.5.cloned.1.call-update) | async-done | bytes 196624 | tf_op jit(solution)/shard_map/while/body/eval_jaxpr/psum | solution.py:29
  122.9 1.6 constant_dynamic-update-slice_fusion.3
  124.5 2.8 %convolution_add_fusion.3 = f32[128,2048]{1,0:T(8,128)} fusion(bf16[384,2048]{1,0:T(8,128)(2,1)S(1)} %copy.12, f32[128,2048]{1,0:T(8,128)} %get-tuple-element.247, pred[]{:T(512)S(6)} %compare.5, f32[128,384]{1,0:T(8,128)} %all-reduce.5.cloned.1.call-done), kind=kOutput, calls=%fused_computation.clone.1 | convolution fusion | flops 201900032 | bytes 3866625 | tf_op jit(solution)/shard_map/while/body/eval_jaxpr/dot_general | solution.py:31
  127.3 2.4 %convolution_bitcast_fusion = f32[128,384]{0,1:T(8,128)} fusion(bf16[384,2048]{1,0:T(8,128)(2,1)S(1)} %get-tuple-element.160, bf16[1,128,2048]{2,1,0:T(8,128)(2,1)} %bitcast.22), kind=kOutput, calls=%fused_computation.6 | convolution fusion | flops 201326592 | bytes 2293760 | tf_op jit(solution)/shard_map/dot_general | solution.py:26
  129.8 31.9 %all-reduce.3.cloned.1.call-done = f32[128,384]{0,1:T(8,128)} async-done(((f32[128,384]{0,1:T(8,128)}), f32[128,384]{0,1:T(8,128)}) %all-reduce.3.cloned.1.call-update) | async-done | bytes 196624 | tf_op jit(solution)/shard_map/psum | solution.py:29
  161.7 1.1 copy.4
  162.7 0.7 constant_dynamic-update-slice_fusion.1
  163.4 2.4 %fusion.2 = f32[1,128,2048]{2,1,0:T(8,128)} fusion(f32[128,2048]{1,0:T(8,128)S(1)} %copy-done.1, bf16[384,2048]{1,0:T(8,128)(2,1)S(1)} %get-tuple-element.160, f32[128,384]{0,1:T(8,128)} %all-reduce.3.cloned.1.call-done, bf16[1,128,2048]{2,1,0:T(8,128)(2,1)S(1)} %bitcast.23), kind=kOutput, calls=%fused_computation.5 | convolution fusion | flops 202162176 | bytes 4390912 | tf_op jit(solution)/shard_map/dot_general | solution.py:31
  (25 shorter events, 1.2 us)
Async XLA Ops:
  8.0 1.7 copy-start
  9.7 34.9 %all-reduce.5.cloned.1.call-start = ((), (), s32[]{:S(2)}) async-start(), calls=%async_computation.1 | async-start | bytes 393216 | tf_op jit(solution)/shard_map/while/body/eval_jaxpr/psum | solution.py:29
  9.7 1.0 copy-start.2
  9.9 38.7 %collective-permute-start = (bf16[384,2048]{1,0:T(8,128)(2,1)S(1)}, bf16[384,2048]{1,0:T(8,128)(2,1)S(1)}, u32[]{:S(2)}, u32[]{:S(2)}) collective-permute-start(bf16[384,2048]{1,0:T(8,128)(2,1)S(1)} %copy.12), channel_id=1, source_target_pairs={{12,0},{0,4},{4,8},{8,12},{13,1},{1,5},{5,9},{9,13},{14,2},{2,6},{... | collective-permute-start | bytes 4718600 | tf_op jit(solution)/shard_map/while/body/eval_jaxpr/ppermute | solution.py:10
  48.6 35.0 %all-reduce.5.cloned.1.call-start = ((), (), s32[]{:S(2)}) async-start(), calls=%async_computation.1 | async-start | bytes 393216 | tf_op jit(solution)/shard_map/while/body/eval_jaxpr/psum | solution.py:29
  48.6 1.0 copy-start.2
  48.7 39.2 %collective-permute-start = (bf16[384,2048]{1,0:T(8,128)(2,1)S(1)}, bf16[384,2048]{1,0:T(8,128)(2,1)S(1)}, u32[]{:S(2)}, u32[]{:S(2)}) collective-permute-start(bf16[384,2048]{1,0:T(8,128)(2,1)S(1)} %copy.12), channel_id=1, source_target_pairs={{12,0},{0,4},{4,8},{8,12},{13,1},{1,5},{5,9},{9,13},{14,2},{2,6},{... | collective-permute-start | bytes 4718600 | tf_op jit(solution)/shard_map/while/body/eval_jaxpr/ppermute | solution.py:10
  87.9 35.0 %all-reduce.5.cloned.1.call-start = ((), (), s32[]{:S(2)}) async-start(), calls=%async_computation.1 | async-start | bytes 393216 | tf_op jit(solution)/shard_map/while/body/eval_jaxpr/psum | solution.py:29
  87.9 1.0 copy-start.2
  88.1 39.2 %collective-permute-start = (bf16[384,2048]{1,0:T(8,128)(2,1)S(1)}, bf16[384,2048]{1,0:T(8,128)(2,1)S(1)}, u32[]{:S(2)}, u32[]{:S(2)}) collective-permute-start(bf16[384,2048]{1,0:T(8,128)(2,1)S(1)} %copy.12), channel_id=1, source_target_pairs={{12,0},{0,4},{4,8},{8,12},{13,1},{1,5},{5,9},{9,13},{14,2},{2,6},{... | collective-permute-start | bytes 4718600 | tf_op jit(solution)/shard_map/while/body/eval_jaxpr/ppermute | solution.py:10
  127.3 34.4 %all-reduce.3.cloned.1.call-start = ((), (), s32[]{:S(2)}) async-start(), calls=%async_computation | async-start | bytes 393216 | tf_op jit(solution)/shard_map/psum | solution.py:29
  127.3 36.1 %copy-start.1 = (f32[128,2048]{1,0:T(8,128)S(1)}, f32[128,2048]{1,0:T(8,128)}, u32[]{:S(2)}) copy-start(f32[128,2048]{1,0:T(8,128)} %get-tuple-element.161) | copy-start | bytes 3145732
  127.3 36.1 %copy-start.3 = (bf16[128,2048]{1,0:T(8,128)(2,1)S(1)}, bf16[128,2048]{1,0:T(8,128)(2,1)}, u32[]{:S(2)}) copy-start(bf16[128,2048]{1,0:T(8,128)(2,1)} %get-tuple-element.272) | copy-start | bytes 1572868
Sparse Core Ops, SparseCore 0:
  12.9 31.6 all-reduce.4
  51.8 31.7 all-reduce.4
  91.2 31.6 all-reduce.4
Sparse Core Ops, SparseCore 1:
  130.1 31.5 all-reduce.2
where the time goes:
time: 176 us; the launch traced here: 173 us
  waiting for transfers between devices  130 us (74%)
  matrix products  16.5 us (9%)
  between operations  15.2 us (9%)
  local copies, waits for them, and re-layouts  10 us (6%)
    psum x4, waiting for transfers between devices, visit(): summed = lax.psum(part, 'pw')  130 us
    dot_general x4, matrix products, visit(): jnp.dot(summed.astype(jnp.bfloat16), piece, preferred_element_type=jnp.fl...  10.2 us
    dot_general x4, matrix products, visit(): lax.dot_general(rows, piece, (((1,), (1,)), ((), ())), preferred_element_...  6.32 us
    dynamic_update_slice x4, local copies, waits for them, and re-layouts, visit(): lax.dynamic_update_slice(correlation, summed, (zero_index, start))  5.54 us
  transfers between devices with their start and end apart: 7, of which 4 were waited for; matrix products, arithmetic and copies ran while one was open for 10% of the time, Pallas kernels for 0%

commit v1 on v0

v1 whole, which is shorter than its diff:
```python
import functools

import jax
import jax.numpy as jnp
from jax import lax
from jax.experimental import pallas as pl
from jax.experimental.pallas import tpu as pltpu
from jax.sharding import PartitionSpec as P

CHUNKS = 4
MESH = pl.DeviceIdType.MESH
NT = (((1,), (1,)), ((), ()))


def kernel(n, width, occ, resp, cout, proj, r_all, cp, rs, wgt, cs, chome, down, narrow, got, last,
           r_send, r_recv, rs_send, rs_recv, ag_send, ag_recv, h_send, h_recv, o_send, o_recv,
           d_send, d_recv, l_recv):
    bands = occ.shape[0]
    rows, cols = resp.shape
    tile = cols // CHUNKS
    me = lax.axis_index("pert")
    mine = lax.axis_index("pw")

    barrier = pltpu.get_barrier_semaphore()
    for k in range(1, n):
        pl.semaphore_signal(barrier, inc=1, device_id={"pert": lax.rem(me + k, n)}, device_id_type=MESH)
    for k in range(1, width):
        pl.semaphore_signal(barrier, inc=1, device_id={"pw": lax.rem(mine + k, width)}, device_id_type=MESH)
    pl.semaphore_wait(barrier, n + width - 2)

    def response_copy(src, q, side):
        return pltpu.make_async_remote_copy(
            src_ref=src, dst_ref=r_all.at[q], send_sem=r_send.at[side, q], recv_sem=r_recv.at[q],
            device_id={"pert": me + 2 * side - 1}, device_id_type=MESH)

    def partial_copy(q, peer):
        return pltpu.make_async_remote_copy(
            src_ref=cp.at[q, peer], dst_ref=rs.at[q, mine], send_sem=rs_send.at[q, peer],
            recv_sem=rs_recv.at[q, mine], device_id={"pw": peer}, device_id_type=MESH)

    def weight_copy(q, peer):
        return pltpu.make_async_remote_copy(
            src_ref=wgt.at[q, mine], dst_ref=wgt.at[q, mine], send_sem=ag_send.at[q, peer],
            recv_sem=ag_recv.at[q, mine], device_id={"pw": peer}, device_id_type=MESH)

    def home_copy(q):
        return pltpu.make_async_remote_copy(
            src_ref=cs.at[q], dst_ref=chome.at[me], send_sem=h_send.at[q], recv_sem=h_recv.at[me],
            device_id={"pert": q}, device_id_type=MESH)

    def spread_copy(j, peer):
        where = cout.at[mine, :, pl.ds(pl.multiple_of(j * bands, 128), bands)]
        return pltpu.make_async_remote_copy(
            src_ref=chome.at[j], dst_ref=where, send_sem=o_send.at[j, peer],
            recv_sem=o_recv.at[j, mine], device_id={"pw": peer}, device_id_type=MESH)

    def narrow_copy(q, c):
        return pltpu.make_async_remote_copy(
            src_ref=narrow.at[q, c], dst_ref=got.at[q, c], send_sem=d_send.at[q, c],
            recv_sem=d_recv.at[q, c], device_id={"pert": jnp.where(q < me, me - 1, me + 1)},
            device_id_type=MESH)

    def last_copy(q, c):
        side = jnp.where(q < me, 0, 1)
        return pltpu.make_async_remote_copy(
            src_ref=down.at[q, c], dst_ref=last.at[side, c], send_sem=d_send.at[q, c],
            recv_sem=l_recv.at[side, c], device_id={"pert": q}, device_id_type=MESH)

    def arrived(ref, sem):
        pltpu.make_async_copy(ref, ref, sem).wait()

    def is_next(q):
        return (q == me - 1) | (q == me + 1)

    def send_correction(q, c, value):
        @pl.when(is_next(q))
        def _():
            down[q, c] = value
            last_copy(q, c).start()

        @pl.when(jnp.logical_not(is_next(q)))
        def _():
            narrow[q, c] = value.astype(narrow.dtype)
            narrow_copy(q, c).start()

    for side in range(2):
        @pl.when((me > 0) if side == 0 else (me < n - 1))
        def _(side=side):
            response_copy(resp, me, side).start()
    r_all[me] = resp[...]

    def process(q):
        part = lax.dot_general(r_all[q], occ[...], NT, preferred_element_type=jnp.float32)
        cp[q] = part.reshape(cp.shape[1:])
        for k in range(1, width):
            partial_copy(q, lax.rem(mine + k, width)).start()
        rs[q, mine] = cp[q, mine]
        for k in range(1, width):
            src = lax.rem(mine + k, width)
            arrived(rs.at[q, src], rs_recv.at[q, src])
        total = rs[q, 0]
        for k in range(1, width):
            total = total + rs[q, k]
        wgt[q, mine] = total.astype(wgt.dtype)
        for k in range(1, width):
            weight_copy(q, lax.rem(mine + k, width)).start()

        @pl.when(q == me)
        def _():
            chome[q] = total

        @pl.when(q != me)
        def _():
            cs[q] = total
            home_copy(q).start()

        for k in range(1, width):
            src = lax.rem(mine + k, width)
            arrived(wgt.at[q, src], ag_recv.at[q, src])
        weights = wgt[q].reshape(rows, bands)
        source = ((q < me) & (me == n - 1)) | ((q > me) & (me == 0))
        for c in range(CHUNKS):
            value = jnp.dot(weights, occ[:, c * tile:(c + 1) * tile], preferred_element_type=jnp.float32)

            @pl.when(source)
            def _(c=c, value=value):
                send_correction(q, c, value)

            @pl.when(jnp.logical_not(source))
            def _(c=c, value=value):
                down[q, c] = value

    def relay(step):
        for c in range(CHUNKS):
            for side in range(2):
                q = n - 1 - step if side == 0 else step
                between = ((q < me) & (me < n - 1)) if side == 0 else ((q > me) & (me > 0))

                @pl.when(between)
                def _(c=c, q=q):
                    arrived(got.at[q, c], d_recv.at[q, c])
                    send_correction(q, c, down[q, c] + got[q, c].astype(jnp.float32))

    def spread(step):
        def one(side, _):
            j = me + step * (2 * side - 1)

            @pl.when((j >= 0) & (j < n) & ((side == 0) | (step > 0)))
            def _():
                @pl.when(j != me)
                def _():
                    arrived(chome.at[j], h_recv.at[j])

                for k in range(1, width):
                    spread_copy(j, lax.rem(mine + k, width)).start()
                cout[mine, :, pl.ds(pl.multiple_of(j * bands, 128), bands)] = chome[j]
            return 0

        lax.fori_loop(0, 2, one, 0)

    def turn(step, _):
        def one(side, _):
            q = me + step * (2 * side - 1)

            @pl.when((q >= 0) & (q < n) & ((side == 0) | (step > 0)))
            def _():
                @pl.when(q != me)
                def _():
                    arrived(r_all.at[q], r_recv.at[q])

                    @pl.when((side == 0) & (me < n - 1))
                    def _():
                        response_copy(r_all.at[q], q, 1).start()

                    @pl.when((side == 1) & (me > 0))
                    def _():
                        response_copy(r_all.at[q], q, 0).start()

                process(q)
            return 0

        lax.fori_loop(0, 2, one, 0)

        @pl.when(step > 0)
        def _():
            relay(step - 1)
            spread(step - 1)
        return 0

    lax.fori_loop(0, n, turn, 0)
    relay(n - 1)
    spread(n - 1)

    for c in range(CHUNKS):
        at = slice(c * tile, (c + 1) * tile)
        proj[:, at] = down[me, c]

        for side in range(2):
            @pl.when((me < n - 1) if side == 0 else (me > 0))
            def _(side=side, at=at, c=c):
                arrived(last.at[side, c], l_recv.at[side, c])
                proj[:, at] = proj[:, at] + last[side, c]

        proj[:, at] = resp[:, at].astype(jnp.float32) - proj[:, at]

    def drain(q, _):
        for k in range(1, width):
            peer = lax.rem(mine + k, width)
            partial_copy(q, peer).wait_send()
            weight_copy(q, peer).wait_send()
            spread_copy(q, peer).wait_send()
            arrived(cout.at[peer, :, pl.ds(pl.multiple_of(q * bands, 128), bands)], o_recv.at[q, peer])

        @pl.when((q >= me) & (me > 0))
        def _():
            response_copy(r_all.at[q], q, 0).wait_send()

        @pl.when((q <= me) & (me < n - 1))
        def _():
            response_copy(r_all.at[q], q, 1).wait_send()

        @pl.when(q != me)
        def _():
            home_copy(q).wait_send()
            for c in range(CHUNKS):
                @pl.when(is_next(q))
                def _(c=c):
                    last_copy(q, c).wait_send()

                @pl.when(jnp.logical_not(is_next(q)))
                def _(c=c):
                    narrow_copy(q, c).wait_send()
        return 0

    lax.fori_loop(0, n, drain, 0)


def fused(occupied, rows):
    n, width = lax.axis_size("pert"), lax.axis_size("pw")
    count, cols = rows.shape
    bands = occupied.shape[0]
    part, tile = count // width, cols // CHUNKS
    f32, bf16 = jnp.float32, jnp.bfloat16
    dma = pltpu.SemaphoreType.DMA
    vmem = pl.BlockSpec(memory_space=pltpu.VMEM)
    correlation, projected = pl.pallas_call(
        functools.partial(kernel, n, width),
        out_shape=(
            jax.ShapeDtypeStruct((width, part, n * bands), f32),
            jax.ShapeDtypeStruct((count, cols), f32),
        ),
        in_specs=[vmem] * 2,
        out_specs=(vmem, vmem),
        scratch_shapes=[
            pltpu.VMEM((n, count, cols), bf16),
            pltpu.VMEM((n, width, part, bands), f32),
            pltpu.VMEM((n, width, part, bands), f32),
            pltpu.VMEM((n, width, part, bands), bf16),
            pltpu.VMEM((n, part, bands), f32),
            pltpu.VMEM((n, part, bands), f32),
            pltpu.VMEM((n, CHUNKS, count, tile), f32),
            pltpu.VMEM((n, CHUNKS, count, tile), bf16),
            pltpu.VMEM((n, CHUNKS, count, tile), bf16),
            pltpu.VMEM((2, CHUNKS, count, tile), f32),
            dma((2, n)), dma((n,)),
            dma((n, width)), dma((n, width)),
            dma((n, width)), dma((n, width)),
            dma((n,)), dma((n,)),
            dma((n, width)), dma((n, width)),
            dma((n, CHUNKS)), dma((n, CHUNKS)), dma((2, CHUNKS)),
        ],
        compiler_params=pltpu.CompilerParams(
            collective_id=0, has_side_effects=True, vmem_limit_bytes=48 * 2**20
        ),
    )(occupied, rows)
    return correlation.reshape(count, n * bands), projected


def ring(occupied, rows):
    band_local = occupied.shape[0]
    n = lax.axis_size("pert")
    position = lax.axis_index("pert")
    zero = jnp.zeros((), jnp.int32)

    def visit(step, piece, correlation, correction):
        start = (position - step) % n * band_local
        part = lax.dot_general(rows, piece, NT, preferred_element_type=jnp.float32)
        summed = lax.psum(part, "pw")
        correlation = lax.dynamic_update_slice(correlation, summed, (zero, start))
        correction = correction + jnp.dot(
            summed.astype(jnp.bfloat16), piece, preferred_element_type=jnp.float32
        )
        return correlation, correction

    def turn(step, state):
        piece, correlation, correction = state
        correlation, correction = visit(step, piece, correlation, correction)
        piece = lax.ppermute(piece, "pert", [(i, (i + 1) % n) for i in range(n)])
        return piece, correlation, correction

    state = (occupied, jnp.zeros((rows.shape[0], n * band_local), jnp.float32), jnp.zeros(rows.shape, jnp.float32))
    piece, correlation, correction = lax.fori_loop(0, n - 1, turn, state)
    correlation, correction = visit(n - 1, piece, correlation, correction)
    return correlation, rows.astype(jnp.float32) - correction


def local(occupied, response):
    rows = response.reshape(-1, response.shape[-1])
    small = rows.shape[0] <= occupied.shape[0]
    even = occupied.shape[0] % 128 == 0 and rows.shape[0] % (16 * lax.axis_size("pw")) == 0
    body = fused if small and even and rows.shape[1] % (128 * CHUNKS) == 0 else ring
    correlation, projected = body(occupied, rows)
    return correlation.reshape(response.shape[:2] + correlation.shape[1:]), projected.reshape(response.shape)


def solution(mesh):
    in_specs = (P(("kpt", "pert"), "pw"), P(("kpt", "pert"), None, "pw"))
    out_specs = (P(("kpt", "pert"), None, None), P(("kpt", "pert"), None, "pw"))
    return jax.shard_map(local, mesh=mesh, in_specs=in_specs, out_specs=out_specs, check_vma=False)
```

time: 176 us -> 119 us (0.68); the launches traced: 173 us -> 118 us
  waiting for transfers between devices: 130 us -> 0 us
  Pallas kernels: 0 us -> 113 us
  matrix products: 16.5 us -> 0 us
  between operations: 15.2 us -> 0.65 us
  local copies, waits for them, and re-layouts: 10 us -> 4.29 us
    psum x4 -> x0, waiting for transfers between devices: 130 us -> none  [visit(): summed = lax.psum(part, 'pw')]
    pallas_call x0 -> x1, Pallas kernels: none -> 113 us  [fused(): pl.pallas_call(functools.partial(kernel, n, width), out_shape=(jax.ShapeD...]
    dot_general x8 -> x0, matrix products: 16.5 us -> none  [the longest x4 10.2 us: visit(): jnp.dot(summed.astype(jnp.bfloat16), piece, preferred_element_type=jnp.fl...]
    dynamic_update_slice x4 -> x0, local copies, waits for them, and re-layouts: 5.54 us -> none  [visit(): lax.dynamic_update_slice(correlation, summed, (zero_index, start))]
    unnamed x6, local copies, waits for them, and re-layouts: 0.72 us -> 4.29 us
  transfers between devices with their start and end apart: 7 -> 0, of which waited for: 4 -> 0; matrix products, arithmetic and copies ran while one was open for 10% -> 0% of each run, Pallas kernels for 0% -> 0%
where the time goes in v1:
time: 119 us; the launch traced here: 118 us
  Pallas kernels  113 us (95%)
  local copies, waits for them, and re-layouts  4.29 us (4%)
    pallas_call x1, Pallas kernels, fused(): pl.pallas_call(functools.partial(kernel, n, width), out_shape=(jax.ShapeD...  113 us
    unnamed x6, local copies, waits for them, and re-layouts  4.29 us

profile of v1, /device:TPU:30, one launch (start us, length us, event | category | flops | bytes accessed | tf_op | source)
XLA Modules:
  0.0 118.2 jit_solution(17652680892412589595)
XLA Ops:
  0.6 0.0 copy-start
  0.6 1.4 %copy-done = bf16[384,2048]{1,0:T(8,128)(2,1)S(1)} copy-done((bf16[384,2048]{1,0:T(8,128)(2,1)S(1)}, bf16[384,2048]{1,0:T(8,128)(2,1)}, u32[]{:S(2)}) %copy-start) | copy-done | bytes 1572888
  2.0 0.0 copy-start.1
  2.0 1.0 copy-done.1
  3.1 113.3 %shard_map.41 = (f32[4,32,1536]{2,1,0:T(8,128)S(1)}, f32[128,2048]{1,0:T(8,128)S(1)}) custom-call(bf16[384,2048]{1,0:T(8,128)(2,1)S(1)} %copy-done, bf16[128,2048]{1,0:T(8,128)(2,1)S(1)} %bitcast.5), custom_call_target="tpu_custom_call" | custom-call | tf_op jit(solution)/shard_map/pallas_call | solution.py:246
  116.4 0.9 copy.6
  117.2 1.0 copy.7
Async XLA Ops:
  0.6 1.4 %copy-start = (bf16[384,2048]{1,0:T(8,128)(2,1)S(1)}, bf16[384,2048]{1,0:T(8,128)(2,1)}, u32[]{:S(2)}) copy-start(bf16[384,2048]{1,0:T(8,128)(2,1)} %occ.1) | copy-start | bytes 4718596
  2.0 1.0 copy-start.1

commit v2 on v1

--- a/solution.py
+++ b/solution.py
@@ -12,25 +12,30 @@
 NT = (((1,), (1,)), ((), ()))
 
 
-def kernel(n, width, occ, resp, cout, proj, r_all, cp, rs, wgt, cs, chome, down, narrow, got, last,
-           r_send, r_recv, rs_send, rs_recv, ag_send, ag_recv, h_send, h_recv, o_send, o_recv,
-           d_send, d_recv, l_recv):
+def kernel(n, width, occ_far, resp_far, cout, proj, occ, r_all, cp, rs, wgt, cs, chome, down, narrow, got,
+           last, in_sem, r_send, r_recv, rs_send, rs_recv, ag_send, ag_recv, h_send, h_recv, o_send, o_recv,
+           d_send, d_recv, f_send, l_recv):
     bands = occ.shape[0]
-    rows, cols = resp.shape
+    rows, cols = resp_far.shape
     tile = cols // CHUNKS
     me = lax.axis_index("pert")
     mine = lax.axis_index("pw")
 
+    bring_rows = pltpu.make_async_copy(resp_far, r_all.at[me], in_sem.at[0])
+    bring_bands = pltpu.make_async_copy(occ_far, occ, in_sem.at[1])
+    bring_rows.start()
+    bring_bands.start()
     barrier = pltpu.get_barrier_semaphore()
     for k in range(1, n):
         pl.semaphore_signal(barrier, inc=1, device_id={"pert": lax.rem(me + k, n)}, device_id_type=MESH)
     for k in range(1, width):
         pl.semaphore_signal(barrier, inc=1, device_id={"pw": lax.rem(mine + k, width)}, device_id_type=MESH)
+    bring_rows.wait()
     pl.semaphore_wait(barrier, n + width - 2)
 
-    def response_copy(src, q, side):
-        return pltpu.make_async_remote_copy(
-            src_ref=src, dst_ref=r_all.at[q], send_sem=r_send.at[side, q], recv_sem=r_recv.at[q],
+    def response_copy(q, side):
+        return pltpu.make_async_remote_copy(
+            src_ref=r_all.at[q], dst_ref=r_all.at[q], send_sem=r_send.at[side, q], recv_sem=r_recv.at[q],
             device_id={"pert": me + 2 * side - 1}, device_id_type=MESH)
 
     def partial_copy(q, peer):
@@ -63,31 +68,26 @@
     def last_copy(q, c):
         side = jnp.where(q < me, 0, 1)
         return pltpu.make_async_remote_copy(
-            src_ref=down.at[q, c], dst_ref=last.at[side, c], send_sem=d_send.at[q, c],
-            recv_sem=l_recv.at[side, c], device_id={"pert": q}, device_id_type=MESH)
+            src_ref=narrow.at[q, c], dst_ref=last.at[side, 0, c], send_sem=d_send.at[q, c],
+            recv_sem=l_recv.at[side, 0, c], device_id={"pert": q}, device_id_type=MESH)
+
+    def forward_copy(q, c):
+        side = jnp.where(q < me, 0, 1)
+        return pltpu.make_async_remote_copy(
+            src_ref=got.at[q, c], dst_ref=last.at[side, 1, c], send_sem=f_send.at[q, c],
+            recv_sem=l_recv.at[side, 1, c], device_id={"pert": q}, device_id_type=MESH)
 
     def arrived(ref, sem):
         pltpu.make_async_copy(ref, ref, sem).wait()
 
     def is_next(q):
         return (q == me - 1) | (q == me + 1)
-
-    def send_correction(q, c, value):
-        @pl.when(is_next(q))
-        def _():
-            down[q, c] = value
-            last_copy(q, c).start()
-
-        @pl.when(jnp.logical_not(is_next(q)))
-        def _():
-            narrow[q, c] = value.astype(narrow.dtype)
-            narrow_copy(q, c).start()
 
     for side in range(2):
         @pl.when((me > 0) if side == 0 else (me < n - 1))
         def _(side=side):
-            response_copy(resp, me, side).start()
-    r_all[me] = resp[...]
+            response_copy(me, side).start()
+    bring_bands.wait()
 
     def process(q):
         part = lax.dot_general(r_all[q], occ[...], NT, preferred_element_type=jnp.float32)
@@ -122,13 +122,32 @@
         for c in range(CHUNKS):
             value = jnp.dot(weights, occ[:, c * tile:(c + 1) * tile], preferred_element_type=jnp.float32)
 
-            @pl.when(source)
+            @pl.when(source | is_next(q))
             def _(c=c, value=value):
-                send_correction(q, c, value)
-
-            @pl.when(jnp.logical_not(source))
+                narrow[q, c] = value.astype(narrow.dtype)
+
+            @pl.when(source & is_next(q))
+            def _(c=c):
+                last_copy(q, c).start()
+
+            @pl.when(source & jnp.logical_not(is_next(q)))
+            def _(c=c):
+                narrow_copy(q, c).start()
+
+            @pl.when(jnp.logical_not(source | is_next(q)))
             def _(c=c, value=value):
                 down[q, c] = value
+
+    def launch(step):
+        for side in range(2):
+            inner = (me > 0) & (me < n - 1)
+            final = n - me if side == 0 else me + 1
+
+            @pl.when(inner & (step == final))
+            def _(side=side):
+                response_copy(n - 1 if side == 0 else 0, side).wait_send()
+                for c in range(CHUNKS):
+                    last_copy(me + 2 * side - 1, c).start()
 
     def relay(step):
         for c in range(CHUNKS):
@@ -139,7 +158,16 @@
                 @pl.when(between)
                 def _(c=c, q=q):
                     arrived(got.at[q, c], d_recv.at[q, c])
-                    send_correction(q, c, down[q, c] + got[q, c].astype(jnp.float32))
+
+                    @pl.when(is_next(q))
+                    def _():
+                        forward_copy(q, c).start()
+
+                    @pl.when(jnp.logical_not(is_next(q)))
+                    def _():
+                        total = down[q, c] + got[q, c].astype(jnp.float32)
+                        narrow[q, c] = total.astype(narrow.dtype)
+                        narrow_copy(q, c).start()
 
     def spread(step):
         def one(side, _):
@@ -159,6 +187,8 @@
         lax.fori_loop(0, 2, one, 0)
 
     def turn(step, _):
+        launch(step)
+
         def one(side, _):
             q = me + step * (2 * side - 1)
 
@@ -170,11 +200,11 @@
 
                     @pl.when((side == 0) & (me < n - 1))
                     def _():
-                        response_copy(r_all.at[q], q, 1).start()
+                        response_copy(q, 1).start()
 
                     @pl.when((side == 1) & (me > 0))
                     def _():
-                        response_copy(r_all.at[q], q, 0).start()
+                        response_copy(q, 0).start()
 
                 process(q)
             return 0
@@ -188,6 +218,7 @@
         return 0
 
     lax.fori_loop(0, n, turn, 0)
+    launch(n)
     relay(n - 1)
     spread(n - 1)
 
@@ -196,12 +227,13 @@
         proj[:, at] = down[me, c]
 
         for side in range(2):
-            @pl.when((me < n - 1) if side == 0 else (me > 0))
-            def _(side=side, at=at, c=c):
-                arrived(last.at[side, c], l_recv.at[side, c])
-                proj[:, at] = proj[:, at] + last[side, c]
-
-        proj[:, at] = resp[:, at].astype(jnp.float32) - proj[:, at]
+            for k in range(2):
+                @pl.when((me < n - 1 - k) if side == 0 else (me > k))
+                def _(side=side, k=k, at=at, c=c):
+                    arrived(last.at[side, k, c], l_recv.at[side, k, c])
+                    proj[:, at] = proj[:, at] + last[side, k, c].astype(jnp.float32)
+
+        proj[:, at] = r_all[me, :, at].astype(jnp.float32) - proj[:, at]
 
     def drain(q, _):
         for k in range(1, width):
@@ -211,13 +243,15 @@
             spread_copy(q, peer).wait_send()
             arrived(cout.at[peer, :, pl.ds(pl.multiple_of(q * bands, 128), bands)], o_recv.at[q, peer])
 
-        @pl.when((q >= me) & (me > 0))
-        def _():
-            response_copy(r_all.at[q], q, 0).wait_send()
-
-        @pl.when((q <= me) & (me < n - 1))
-        def _():
-            response_copy(r_all.at[q], q, 1).wait_send()
+        inner = (me > 0) & (me < n - 1)
+
+        @pl.when((q >= me) & (me > 0) & jnp.logical_not(inner & (q == n - 1)))
+        def _():
+            response_copy(q, 0).wait_send()
+
+        @pl.when((q <= me) & (me < n - 1) & jnp.logical_not(inner & (q == 0)))
+        def _():
+            response_copy(q, 1).wait_send()
 
         @pl.when(q != me)
         def _():
@@ -226,6 +260,10 @@
                 @pl.when(is_next(q))
                 def _(c=c):
                     last_copy(q, c).wait_send()
+
+                    @pl.when(inner)
+                    def _():
+                        forward_copy(q, c).wait_send()
 
                 @pl.when(jnp.logical_not(is_next(q)))
                 def _(c=c):
@@ -249,9 +287,10 @@
             jax.ShapeDtypeStruct((width, part, n * bands), f32),
             jax.ShapeDtypeStruct((count, cols), f32),
         ),
-        in_specs=[vmem] * 2,
+        in_specs=[pl.BlockSpec(memory_space=pltpu.HBM)] * 2,
         out_specs=(vmem, vmem),
         scratch_shapes=[
+            pltpu.VMEM((bands, cols), bf16),
             pltpu.VMEM((n, count, cols), bf16),
             pltpu.VMEM((n, width, part, bands), f32),
             pltpu.VMEM((n, width, part, bands), f32),
@@ -261,13 +300,13 @@
             pltpu.VMEM((n, CHUNKS, count, tile), f32),
             pltpu.VMEM((n, CHUNKS, count, tile), bf16),
             pltpu.VMEM((n, CHUNKS, count, tile), bf16),
-            pltpu.VMEM((2, CHUNKS, count, tile), f32),
-            dma((2, n)), dma((n,)),
+            pltpu.VMEM((2, 2, CHUNKS, count, tile), bf16),
+            dma((2,)), dma((2, n)), dma((n,)),
             dma((n, width)), dma((n, width)),
             dma((n, width)), dma((n, width)),
             dma((n,)), dma((n,)),
             dma((n, width)), dma((n, width)),
-            dma((n, CHUNKS)), dma((n, CHUNKS)), dma((2, CHUNKS)),
+            dma((n, CHUNKS)), dma((n, CHUNKS)), dma((n, CHUNKS)), dma((2, 2, CHUNKS)),
         ],
         compiler_params=pltpu.CompilerParams(
             collective_id=0, has_side_effects=True, vmem_limit_bytes=48 * 2**20

time: 119 us -> 106 us (0.89)
  Pallas kernels: 113 us -> 101 us
    pallas_call x1, Pallas kernels: 113 us -> 101 us  [fused(): pl.pallas_call(functools.partial(kernel, n, width), out_shape=(jax.ShapeD...]
where the time goes in v2:
time: 106 us
  Pallas kernels  101 us (95%)
  local copies, waits for them, and re-layouts  4.29 us (4%)
    pallas_call x1, Pallas kernels, fused(): pl.pallas_call(functools.partial(kernel, n, width), out_shape=(jax.ShapeD...  101 us
    unnamed x6, local copies, waits for them, and re-layouts  4.29 us

profile of v2, /device:TPU:30, one launch (start us, length us, event | category | flops | bytes accessed | tf_op | source)
XLA Modules:
  0.0 105.8 jit_solution(17234561692083246394)
XLA Ops:
  0.6 0.0 copy-start
  0.6 1.4 %copy-done = bf16[384,2048]{1,0:T(8,128)(2,1)S(1)} copy-done((bf16[384,2048]{1,0:T(8,128)(2,1)S(1)}, bf16[384,2048]{1,0:T(8,128)(2,1)}, u32[]{:S(2)}) %copy-start) | copy-done | bytes 1572888
  2.0 0.0 copy-start.1
  2.0 1.0 copy-done.1
  3.1 100.8 %shard_map.41 = (f32[4,32,1536]{2,1,0:T(8,128)S(1)}, f32[128,2048]{1,0:T(8,128)S(1)}) custom-call(bf16[384,2048]{1,0:T(8,128)(2,1)S(1)} %copy-done, bf16[128,2048]{1,0:T(8,128)(2,1)S(1)} %bitcast.5), custom_call_target="tpu_custom_call" | custom-call | tf_op jit(solution)/shard_map/pallas_call | solution.py:284
  103.9 0.9 copy.6
  104.8 1.0 copy.7
Async XLA Ops:
  0.6 1.4 %copy-start = (bf16[384,2048]{1,0:T(8,128)(2,1)S(1)}, bf16[384,2048]{1,0:T(8,128)(2,1)}, u32[]{:S(2)}) copy-start(bf16[384,2048]{1,0:T(8,128)(2,1)} %occ_far.1) | copy-start | bytes 4718596
  2.0 1.0 copy-start.1

commit v3 on v2

--- a/solution.py
+++ b/solution.py
@@ -7,7 +7,7 @@
 from jax.experimental.pallas import tpu as pltpu
 from jax.sharding import PartitionSpec as P
 
-CHUNKS = 4
+CHUNKS = 2
 MESH = pl.DeviceIdType.MESH
 NT = (((1,), (1,)), ((), ()))
 
@@ -89,12 +89,14 @@
             response_copy(me, side).start()
     bring_bands.wait()
 
-    def process(q):
+    def multiply(q):
         part = lax.dot_general(r_all[q], occ[...], NT, preferred_element_type=jnp.float32)
         cp[q] = part.reshape(cp.shape[1:])
         for k in range(1, width):
             partial_copy(q, lax.rem(mine + k, width)).start()
         rs[q, mine] = cp[q, mine]
+
+    def total_up(q):
         for k in range(1, width):
             src = lax.rem(mine + k, width)
             arrived(rs.at[q, src], rs_recv.at[q, src])
@@ -114,6 +116,7 @@
             cs[q] = total
             home_copy(q).start()
 
+    def correct(q):
         for k in range(1, width):
             src = lax.rem(mine + k, width)
             arrived(wgt.at[q, src], ag_recv.at[q, src])
@@ -189,27 +192,34 @@
     def turn(step, _):
         launch(step)
 
-        def one(side, _):
-            q = me + step * (2 * side - 1)
-
-            @pl.when((q >= 0) & (q < n) & ((side == 0) | (step > 0)))
+        def each(stage):
+            def one(side, _):
+                q = me + step * (2 * side - 1)
+
+                @pl.when((q >= 0) & (q < n) & ((side == 0) | (step > 0)))
+                def _():
+                    stage(q, side)
+                return 0
+
+            lax.fori_loop(0, 2, one, 0)
+
+        def receive(q, side):
+            @pl.when(q != me)
             def _():
-                @pl.when(q != me)
+                arrived(r_all.at[q], r_recv.at[q])
+
+                @pl.when((side == 0) & (me < n - 1))
                 def _():
-                    arrived(r_all.at[q], r_recv.at[q])
-
-                    @pl.when((side == 0) & (me < n - 1))
-                    def _():
-                        response_copy(q, 1).start()
-
-                    @pl.when((side == 1) & (me > 0))
-                    def _():
-                        response_copy(q, 0).start()
-
-                process(q)
-            return 0
-
-        lax.fori_loop(0, 2, one, 0)
+                    response_copy(q, 1).start()
+
+                @pl.when((side == 1) & (me > 0))
+                def _():
+                    response_copy(q, 0).start()
+
+        each(receive)
+        each(lambda q, side: multiply(q))
+        each(lambda q, side: total_up(q))
+        each(lambda q, side: correct(q))
 
         @pl.when(step > 0)
         def _():

time: 106 us -> 93 us (0.88)
  Pallas kernels: 101 us -> 87.8 us
    pallas_call x1, Pallas kernels: 101 us -> 87.8 us  [fused(): pl.pallas_call(functools.partial(kernel, n, width), out_shape=(jax.ShapeD...]
where the time goes in v3:
time: 93 us; the launch traced here: 92.8 us
  Pallas kernels  87.8 us (94%)
  local copies, waits for them, and re-layouts  4.29 us (5%)
    pallas_call x1, Pallas kernels, fused(): pl.pallas_call(functools.partial(kernel, n, width), out_shape=(jax.ShapeD...  87.8 us
    unnamed x6, local copies, waits for them, and re-layouts  4.29 us

profile of v3, /device:TPU:30, one launch (start us, length us, event | category | flops | bytes accessed | tf_op | source)
XLA Modules:
  0.0 92.8 jit_solution(18361262300464256377)
XLA Ops:
  0.6 0.0 copy-start
  0.6 1.4 %copy-done = bf16[384,2048]{1,0:T(8,128)(2,1)S(1)} copy-done((bf16[384,2048]{1,0:T(8,128)(2,1)S(1)}, bf16[384,2048]{1,0:T(8,128)(2,1)}, u32[]{:S(2)}) %copy-start) | copy-done | bytes 1572888
  2.0 0.0 copy-start.1
  2.0 1.0 %copy-done.1 = bf16[1,128,2048]{2,1,0:T(8,128)(2,1)S(1)} copy-done((bf16[1,128,2048]{2,1,0:T(8,128)(2,1)S(1)}, bf16[1,128,2048]{2,1,0:T(8,128)(2,1)}, u32[]{:S(2)}) %copy-start.1) | copy-done | bytes 524312
  3.1 87.8 %shard_map.41 = (f32[4,32,1536]{2,1,0:T(8,128)S(1)}, f32[128,2048]{1,0:T(8,128)S(1)}) custom-call(bf16[384,2048]{1,0:T(8,128)(2,1)S(1)} %copy-done, bf16[128,2048]{1,0:T(8,128)(2,1)S(1)} %bitcast.5), custom_call_target="tpu_custom_call" | custom-call | tf_op jit(solution)/shard_map/pallas_call | solution.py:294
  90.9 0.9 copy.6
  91.8 1.0 %copy.7 = f32[1,128,2048]{2,1,0:T(8,128)} copy(f32[1,128,2048]{2,1,0:T(8,128)S(1)} %bitcast.3) | data formatting | bytes 2097152
Async XLA Ops:
  0.6 1.4 %copy-start = (bf16[384,2048]{1,0:T(8,128)(2,1)S(1)}, bf16[384,2048]{1,0:T(8,128)(2,1)}, u32[]{:S(2)}) copy-start(bf16[384,2048]{1,0:T(8,128)(2,1)} %occ_far.1) | copy-start | bytes 4718596
  2.0 1.0 %copy-start.1 = (bf16[1,128,2048]{2,1,0:T(8,128)(2,1)S(1)}, bf16[1,128,2048]{2,1,0:T(8,128)(2,1)}, u32[]{:S(2)}) copy-start(bf16[1,128,2048]{2,1,0:T(8,128)(2,1)} %param.3) | copy-start | bytes 1572868

commit v4 on v3

--- a/solution.py
+++ b/solution.py
@@ -319,7 +319,7 @@
             dma((n, CHUNKS)), dma((n, CHUNKS)), dma((n, CHUNKS)), dma((2, 2, CHUNKS)),
         ],
         compiler_params=pltpu.CompilerParams(
-            collective_id=0, has_side_effects=True, vmem_limit_bytes=48 * 2**20
+            collective_id=0, has_side_effects=True, vmem_limit_bytes=51 * 2**20
         ),
     )(occupied, rows)
     return correlation.reshape(count, n * bands), projected

time: 93 us -> 91.3 us (0.982)
  local copies, waits for them, and re-layouts: 4.29 us -> 2.89 us
    unnamed x6 -> x4, local copies, waits for them, and re-layouts: 4.29 us -> 2.89 us
where the time goes in v4:
time: 91.3 us; the launch traced here: 91.1 us
  Pallas kernels  87.5 us (96%)
  local copies, waits for them, and re-layouts  2.89 us (3%)
    pallas_call x1, Pallas kernels, fused(): pl.pallas_call(functools.partial(kernel, n, width), out_shape=(jax.ShapeD...  87.5 us
    unnamed x4, local copies, waits for them, and re-layouts  2.89 us

profile of v4, /device:TPU:30, one launch (start us, length us, event | category | flops | bytes accessed | tf_op | source)
XLA Modules:
  0.0 91.1 jit_solution(7199618603524648997)
XLA Ops:
  0.6 0.0 copy-start
  0.6 1.0 %copy-done = bf16[1,128,2048]{2,1,0:T(8,128)(2,1)S(1)} copy-done((bf16[1,128,2048]{2,1,0:T(8,128)(2,1)S(1)}, bf16[1,128,2048]{2,1,0:T(8,128)(2,1)}, u32[]{:S(2)}) %copy-start) | copy-done | bytes 524312
  1.7 87.5 %shard_map.41 = (f32[4,32,1536]{2,1,0:T(8,128)S(1)}, f32[128,2048]{1,0:T(8,128)S(1)}) custom-call(bf16[384,2048]{1,0:T(8,128)(2,1)} %occ_far.1, bf16[128,2048]{1,0:T(8,128)(2,1)S(1)} %bitcast.5), custom_call_target="tpu_custom_call" | custom-call | tf_op jit(solution)/shard_map/pallas_call | solution.py:294
  89.2 0.9 copy.6
  90.1 1.0 %copy.7 = f32[1,128,2048]{2,1,0:T(8,128)} copy(f32[1,128,2048]{2,1,0:T(8,128)S(1)} %bitcast.3) | data formatting | bytes 2097152
Async XLA Ops:
  0.6 1.0 %copy-start = (bf16[1,128,2048]{2,1,0:T(8,128)(2,1)S(1)}, bf16[1,128,2048]{2,1,0:T(8,128)(2,1)}, u32[]{:S(2)}) copy-start(bf16[1,128,2048]{2,1,0:T(8,128)(2,1)} %param.3) | copy-start | bytes 1572868
